TPU v7x, 32 devices: a whole 2x2x4 slice. The times are simulated.
32 devices in a mesh: group: 8 (over z, x), tensor: 4 (over y, core).
Axes of the slice: x: 2, y: 2, z: 4, core: 2. Of those that a mesh axis runs over, the one named last changes fastest.
Arguments:
- student_in: bfloat16 [1536, 1280], P('group'), may hold values from -6 to 6
- teacher_feat: bfloat16 [1536, 1536], P('group', 'tensor'), may hold values from -6 to 6
- owner: int32 [1536], replicated, may hold values from 0 to 7, as said below
- slot_row: int32 [1536], replicated, may hold values from 0 to 191, as said below
- w_up: bfloat16 [1280, 5120], P(None, 'tensor'), may hold values from -0.15625 to 0.15625
- b_up: float32 [5120], P('tensor'), may hold values from -4 to 4
- w_down: bfloat16 [5120, 1280], P('tensor'), may hold values from -0.078125 to 0.078125
- w_adapt: bfloat16 [1280, 1536], P(None, 'tensor'), may hold values from -0.15625 to 0.15625
Outputs:
- grad_adapt: float32 [1280, 1536], P(None, 'tensor')
- input_grad: bfloat16 [1536, 1280], P('group')
Inputs may be any that keep to these rules, and one draw needn't show every extreme that they name: Every owner receives exactly 192 rows; the rows of one device name one owner at most 24 times, and some owner exactly 24 times. The pairs (owner, slot_row) of all rows are all different.
All inputs are finite; a program needn't handle non-finite values.
Results may differ from a plain program's by a relative error of at most 0.0085.
Values may be sent and summed in bfloat16 or wider, within the bound.
A program may use at most 64 MiB of HBM per device.

v0:
```python
import math

import jax
import jax.numpy as jnp
from jax import lax
from jax.sharding import PartitionSpec as P

RUN = 2


def normalize(values):
    center = jnp.mean(values, axis=-1, keepdims=True)
    spread = jnp.mean(jnp.square(values - center), axis=-1, keepdims=True)
    return (values - center) * lax.rsqrt(spread + 1e-06)


def activate(values):
    return jax.nn.gelu(values, approximate=True)


def tensor_total(partial_value, finisher):
    summed = lax.psum(partial_value, "tensor")
    return finisher(summed, 0)


def per_device(student_in, teacher_feat, owner, slot_row, w_up, b_up, w_down, w_adapt):
    groups = lax.axis_size("group")
    own_index = lax.axis_index("group")
    tok_rows = student_in.shape[0]
    feat_width = teacher_feat.shape[1]
    run_count = tok_rows // RUN
    slot_count = RUN * ((run_count + groups - 1) // groups)
    own_routes = lax.dynamic_slice_in_dim(owner, own_index * tok_rows, tok_rows, 0)
    one_hot = (own_routes[:, None] == jnp.arange(groups, dtype=jnp.int32)[None, :]).astype(
        jnp.int32
    )
    slot_rank = jnp.sum((jnp.cumsum(one_hot, axis=0) - 1) * one_hot, axis=1)
    slot_place = own_routes * slot_count + slot_rank
    outgoing = (
        jnp.zeros((groups * slot_count, feat_width), jnp.bfloat16).at[slot_place].set(teacher_feat)
    )
    incoming = lax.all_to_all(
        outgoing.reshape(groups, slot_count, feat_width),
        "group",
        split_axis=0,
        concat_axis=0,
        tiled=True,
    )
    incoming = incoming.reshape(groups * slot_count, feat_width)
    is_mine = (owner == own_index).reshape(groups, tok_rows).astype(jnp.int32)
    source_slot = (
        jnp.arange(groups, dtype=jnp.int32)[:, None] * slot_count + jnp.cumsum(is_mine, axis=1) - 1
    ).reshape(-1)
    dest_index = jnp.where(is_mine.reshape(-1) > 0, slot_row, tok_rows)
    picked_slot = jnp.zeros((tok_rows,), jnp.int32).at[dest_index].set(source_slot, mode="drop")
    target = incoming[picked_slot]
    x_float = student_in.astype(jnp.float32)
    normed = normalize(x_float).astype(jnp.bfloat16)
    pre_act = jnp.dot(normed, w_up, preferred_element_type=jnp.float32) + b_up
    hidden = activate(pre_act).astype(jnp.bfloat16)

    def add_input(summed, first_row):
        return (x_float + summed).astype(jnp.bfloat16)

    student_out = tensor_total(
        jnp.dot(hidden, w_down, preferred_element_type=jnp.float32), add_input
    )
    adapted = jnp.dot(student_out, w_adapt, preferred_element_type=jnp.float32)
    delta_adapt = (adapted - target.astype(jnp.float32)).astype(jnp.bfloat16)
    grad_part = jnp.dot(student_out.T, delta_adapt, preferred_element_type=jnp.float32) / math.sqrt(
        tok_rows * groups
    )
    grad_adapt = lax.psum(grad_part, "group")

    def round_rows(summed, first_row):
        return summed.astype(jnp.bfloat16)

    grad_out = tensor_total(
        jnp.dot(delta_adapt, w_adapt.T, preferred_element_type=jnp.float32), round_rows
    )
    grad_hidden = jnp.dot(grad_out, w_down.T, preferred_element_type=jnp.float32)
    forward_value, gelu_back = jax.vjp(activate, pre_act)
    grad_pre = gelu_back(grad_hidden)[0].astype(jnp.bfloat16)

    def finish_input(summed, first_row):
        forward_norm, norm_back = jax.vjp(normalize, x_float)
        return (grad_out.astype(jnp.float32) + norm_back(summed)[0]).astype(jnp.bfloat16)

    input_grad = tensor_total(
        jnp.dot(grad_pre, w_up.T, preferred_element_type=jnp.float32), finish_input
    )
    return (grad_adapt, input_grad)


def solution(mesh):
    return jax.shard_map(
        per_device,
        mesh=mesh,
        in_specs=(
            P("group", None),
            P("group", "tensor"),
            P(),
            P(),
            P(None, "tensor"),
            P("tensor"),
            P("tensor", None),
            P(None, "tensor"),
        ),
        out_specs=(P(None, "tensor"), P("group", None)),
        check_vma=False,
    )
```

profile of v0, /device:TPU:0, one launch (start us, length us, event | category | flops | bytes accessed | tf_op | source)
XLA Modules:
  0.0 245.4 jit_solution(16353561751255811734)
XLA Ops:
  7.2 0.9 dynamic_slice.3
  8.1 0.6 reduce-window.14
  8.7 0.2 slice_reduce_fusion.1
  9.0 0.1 add_bitcast_fusion.1
  9.1 0.8 compare_select_fusion.2
  9.9 2.2 scatter_custom_fusion
  12.1 7.2 %all-to-all-start = ((bf16[8,24,384]{2,1,0:T(8,128)(2,1)}), bf16[8,24,384]{2,1,0:T(8,128)(2,1)S(1)}, u32[]{:S(2)}, u32[]{:S(2)}) async-start(bf16[8,24,384]{2,1,0:T(8,128)(2,1)} %bitcast.24), calls=%async_computation | async-start | bytes 294912 | tf_op jit(solution)/shard_map/all_to_all | solution.py:42
  19.4 1.2 convert_reduce_fusion
  20.6 1.3 fusion.17
  21.9 2.9 %convolution_add_fusion = f32[192,1280]{1,0:T(8,128)S(1)} fusion(bf16[1280,1280]{1,0:T(8,128)(2,1)} %param.12, bf16[192,1280]{1,0:T(8,128)(2,1)} %param.8, f32[1280]{0:T(1024)} %param.13, f32[192]{0:T(256)S(1)} %fusion.48, f32[192]{0:T(256)S(1)} %broadcast_multiply_fusion), kind=kOutput, calls=%fused_computation.4 | convolution fusion | flops 630374400 | bytes 4758016 | tf_op jit(solution)/shard_map/dot_general | solution.py:59
  24.8 1.0 copy-done.4
  25.8 1.9 fusion.21
  27.8 0.1 convert_element_type.44
  27.9 0.6 reduce-window.16
  28.5 0.2 slice_reduce_fusion
  28.7 0.1 add_bitcast_fusion
  28.8 0.1 fusion.45
  28.9 0.1 reshape.102
  28.9 6.2 %scatter_custom_fusion.1 = s32[192]{0:T(256)S(1)} fusion(s32[1536]{0:T(1024)S(1)} %get-tuple-element.4, s32[1536]{0:T(1024)S(1)} %reshape.102, s32[]{:T(128)} %constant.55.clone.1), kind=kCustom, calls=%fused_computation.76 | custom fusion | bytes 772 | tf_op jit(solution)/shard_map/scatter | solution.py:55
  35.2 1.7 gather_fusion
  36.8 28.1 %all-reduce.7.cloned.1.call-done = f32[192,1280]{1,0:T(8,128)} async-done(((f32[192,1280]{1,0:T(8,128)}), f32[192,1280]{1,0:T(8,128)}) %all-reduce.7.cloned.1.call-update) | async-done | bytes 983056 | tf_op jit(solution)/shard_map/psum | solution.py:22
  64.9 2.1 fusion.4
  67.1 1.4 fusion.63
  68.5 22.6 %all-reduce.12 = bf16[192,1280]{1,0:T(8,128)(2,1)} all-reduce(f32[192,1280]{1,0:T(8,128)} %fusion.63), channel_id=1, replica_groups=mesh['group'=8,'tensor'=4] {'tensor'}, use_global_device_ids=true, to_apply=%region_11.12 | all-reduce | flops 245760 | bytes 1474560 | tf_op jit(solution)/shard_map/psum | solution.py:22
  91.1 5.9 %fusion.23 = f32[192,1280]{1,0:T(8,128)} fusion(bf16[1280,1280]{1,0:T(8,128)(2,1)} %param.12, f32[192,1280]{1,0:T(8,128)} %copy-done.4, bf16[1280,1280]{1,0:T(8,128)(2,1)S(1)} %copy-done, bf16[192,1280]{1,0:T(8,128)(2,1)} %all-reduce.12), kind=kOutput, calls=%fused_computation.35 | convolution fusion | flops 1263206400 | bytes 9011200 | tf_op jit(solution)/shard_map/dot_general | solution.py:90
  97.0 3.1 %convolution_multiply_fusion = f32[1280,384]{1,0:T(8,128)} fusion(bf16[192,384]{1,0:T(8,128)(2,1)S(1)} %fusion.4, f32[192,1280]{1,0:T(8,128)} %all-reduce.7.cloned.1.call-done, bf16[192,1280]{1,0:T(8,128)(2,1)} %param.8), kind=kOutput, calls=%fused_computation.3 | convolution fusion | flops 189972480 | bytes 3588096 | tf_op jit(solution)/shard_map/dot_general | solution.py:70
  100.2 33.0 %all-reduce.11.cloned.1.call-done = f32[192,1280]{1,0:T(8,128)} async-done(((f32[192,1280]{1,0:T(8,128)}), f32[192,1280]{1,0:T(8,128)}) %all-reduce.11.cloned.1.call-update) | async-done | bytes 983056 | tf_op jit(solution)/shard_map/psum | solution.py:22
  133.2 1.7 multiply_reduce_fusion
  134.9 1.3 fusion.5
  136.2 2.6 %fusion.9 = bf16[192,1280]{1,0:T(8,128)(2,1)} fusion(bf16[192,1280]{1,0:T(8,128)(2,1)} %param.8, f32[192,1280]{1,0:T(8,128)} %all-reduce.11.cloned.1.call-done, f32[192]{0:T(256)S(1)} %add_multiply_fusion, f32[192]{0:T(256)S(1)} %multiply_multiply_fusion.2, f32[192]{0:T(256)S(1)} %fusion.48, f32[192]{0:T(256)S(1)} %broadcast_multiply_fusion, ...), kind=kLoop, calls=%fused_computation.20 | loop fusion | flops 2211840 | bytes 2460672 | tf_op jit(solution)/shard_map/convert_element_type | solution.py:87
  138.8 97.1 %all-reduce.9.cloned.1.call-done = f32[1280,384]{1,0:T(8,128)} async-done(((f32[1280,384]{1,0:T(8,128)}), f32[1280,384]{1,0:T(8,128)}) %all-reduce.9.cloned.1.call-update) | async-done | bytes 1966096 | tf_op jit(solution)/shard_map/psum | solution.py:73
  235.9 2.9 %copy.15 = f32[1280,384]{1,0:T(8,128)} copy(f32[1280,384]{1,0:T(8,128)} %all-reduce.9.cloned.1.call-done) | data formatting | bytes 3932160
  (32 shorter events, 0.4 us)
Async XLA Ops:
  7.2 18.6 %copy-start = (bf16[1280,1280]{1,0:T(8,128)(2,1)S(1)}, bf16[1280,1280]{1,0:T(8,128)(2,1)}, u32[]{:S(2)}) copy-start(bf16[1280,1280]{1,0:T(8,128)(2,1)} %param.14) | copy-start | bytes 9830404
  12.1 23.1 %all-to-all-start = ((bf16[8,24,384]{2,1,0:T(8,128)(2,1)}), bf16[8,24,384]{2,1,0:T(8,128)(2,1)S(1)}, u32[]{:S(2)}, u32[]{:S(2)}) async-start(bf16[8,24,384]{2,1,0:T(8,128)(2,1)} %bitcast.24), calls=%async_computation | async-start | bytes 294912 | tf_op jit(solution)/shard_map/all_to_all | solution.py:42
  19.3 45.6 %all-reduce.7.cloned.1.call-start = ((), (), s32[]{:S(2)}) async-start(), calls=%async_computation.1 | async-start | bytes 1966080 | tf_op jit(solution)/shard_map/psum | solution.py:22
  24.8 1.0 copy-start.4
  25.8 2.0 copy-start.2
  25.8 2.0 copy-start.3
  27.7 105.5 %all-reduce.11.cloned.1.call-start = ((), (), s32[]{:S(2)}) async-start(), calls=%async_computation.3 | async-start | bytes 1966080 | tf_op jit(solution)/shard_map/psum | solution.py:22
  64.9 2.2 copy-start.1
  97.0 138.9 %all-reduce.9.cloned.1.call-start = ((), (), s32[]{:S(2)}) async-start(), calls=%async_computation.2 | async-start | bytes 3932160 | tf_op jit(solution)/shard_map/psum | solution.py:73
Sparse Core Ops, SparseCore 0:
  27.8 37.0 all-reduce.6
  97.1 36.0 all-reduce.10
  137.3 98.5 all-reduce.8
where the time goes:
time: 246 us; the launch traced here: 245 us
  waiting for transfers between devices  158 us (64%)
  blocking collectives  22.6 us (9%)
  matrix products  17.4 us (7%)
  local copies, waits for them, and re-layouts  15.5 us (6%)
  between operations  13.9 us (6%)
  other arithmetic  10.4 us (4%)
  starting transfers between devices  7.35 us (3%)
    psum x1, waiting for transfers between devices, per_device(): grad_adapt = lax.psum(grad_part, 'group')  97.1 us
    psum x2, waiting for transfers between devices, tensor_total(): summed = lax.psum(partial_value, 'tensor')  61.1 us
    psum x1, blocking collectives, tensor_total(): summed = lax.psum(partial_value, 'tensor')  22.6 us
    all_to_all x1, starting transfers between devices, per_device(): lax.all_to_all(outgoing.reshape(groups, slot_count, feat_width), 'group',...  7.23 us
    scatter x1, local copies, waits for them, and re-layouts, per_device(): jnp.zeros((tok_rows,), jnp.int32).at[dest_index]  6.18 us
    dot_general x1, matrix products, per_device(): jnp.dot(grad_pre, w_up.T, preferred_element_type=jnp.float32)  5.85 us
  transfers between devices with their start and end apart: 4, of which 3 were waited for; matrix products, arithmetic and copies ran while one was open for 10% of the time, Pallas kernels for 0%

commit v1 on v0

v1 whole, which is shorter than its diff:
```python
import math

import jax
import jax.numpy as jnp
from jax import lax
from jax.experimental import pallas as pl
from jax.experimental.pallas import tpu as pltpu
from jax.sharding import PartitionSpec as P

RUN = 2
MESH = pl.DeviceIdType.MESH
F32 = jnp.float32
BF16 = jnp.bfloat16
NN = (((1,), (0,)), ((), ()))
NT = (((1,), (1,)), ((), ()))
TN = (((0,), (0,)), ((), ()))
GELU_K = math.sqrt(2.0 / math.pi)
GELU_A = 0.044715


def mm(a, b, dims=NN):
    return lax.dot_general(a, b, dims, preferred_element_type=F32)


def make_kernel(groups, tensors, tok, d, ff, fw, reduce_groups):
    ny = tensors // 2
    half = tok // 2
    cw = 256
    uw = math.gcd(ff, 256)
    nc = d // cw
    slots = RUN * ((tok // RUN + groups - 1) // groups)
    slots = 16 * ((slots + 15) // 16)
    nz = groups // 2
    blk = d // groups if reduce_groups else 8
    scale = 1.0 / math.sqrt(tok * groups)

    def kernel(
        x_ref, teach_ref, owner_ref, slot_ref, b_ref, wup_hbm, wdn_hbm, wad_hbm,
        ga_ref, ig_ref,
        wup, wdn, wad, wsem,
        normed, hidden, dgelu, full, part, send1, recv1, ybuf,
        s1_s, s1_r, y_s, y_r, ag_s, ag_r,
        outgoing, incoming, qt, t_s, t_r,
        adapted, delta, gh, gpre, gtot,
        gp, xsend, xrecv, zsend, zrecv, gfull, gx_s, gx_r, gz_s, gz_r, az_s, az_r, ax_s, ax_r,
        oscr, o_s, o_r,
    ):
        g = lax.axis_index("group")
        t = lax.axis_index("tensor")
        core = lax.rem(t, 2)
        y = lax.div(t, 2)
        mate = t + 1 - 2 * core
        own0 = pl.multiple_of(core * half, 16)
        oth0 = pl.multiple_of((1 - core) * half, 16)
        own = pl.ds(own0, half)
        oth = pl.ds(oth0, half)

        barrier = pltpu.get_barrier_semaphore()
        for k in range(1, tensors):
            pl.semaphore_signal(barrier, inc=1, device_id=(g, lax.rem(t + k, tensors)), device_id_type=MESH)
        for k in range(1, groups):
            pl.semaphore_signal(barrier, inc=1, device_id=(lax.rem(g + k, groups), t), device_id_type=MESH)

        loads = [
            pltpu.make_async_copy(src, dst, wsem.at[i])
            for i, (src, dst) in enumerate(((wup_hbm, wup), (wdn_hbm, wdn), (wad_hbm, wad)))
        ]
        for c in loads:
            c.start()

        sends = []

        def remote(src, dst, ss, rs, dev):
            c = pltpu.make_async_remote_copy(
                src_ref=src, dst_ref=dst, send_sem=ss, recv_sem=rs, device_id=dev, device_id_type=MESH
            )
            c.start()
            sends.append(c)
            return c

        xf = x_ref[...].astype(F32)
        cen = jnp.mean(xf, axis=-1, keepdims=True)
        dev_ = xf - cen
        rstd = lax.rsqrt(jnp.mean(jnp.square(dev_), axis=-1, keepdims=True) + 1e-06)
        normed[...] = (dev_ * rstd).astype(BF16)
        loads[0].wait()
        for j in range(ff // uw):
            cs = slice(j * uw, (j + 1) * uw)
            pre = mm(normed[...], wup[:, cs]) + b_ref[:, cs]
            sq = pre * pre
            th = jnp.tanh(GELU_K * pre * (1.0 + GELU_A * sq))
            hidden[:, cs] = (0.5 * pre * (1.0 + th)).astype(BF16)
            dgelu[:, cs] = 0.5 * (1.0 + th) + 0.5 * GELU_K * pre * (1.0 - th * th) * (1.0 + 3.0 * GELU_A * sq)

        pl.semaphore_wait(barrier, tensors - 1 + groups - 1)
        loads[1].wait()

        state = {}

        def stage1(a, j, value):
            part[a, j] = value
            send1[a, j] = part[a, j, oth, :].astype(BF16)
            state["s1", a, j] = remote(
                send1.at[a, j], recv1.at[a, j], s1_s.at[a, j], s1_r.at[a, j], (g, mate)
            )

        def stage2(a, j):
            state["s1", a, j].wait_recv()
            ybuf[a, j, y] = (part[a, j, own, :] + recv1[a, j].astype(F32)).astype(BF16)
            state["y", a, j] = [
                remote(
                    ybuf.at[a, j, y], ybuf.at[a, j, y], y_s.at[a, j, k - 1], y_r.at[a, j, k - 1],
                    (g, lax.rem(y + k, ny) * 2 + core),
                )
                for k in range(1, ny)
            ]

        def total(a, j):
            for c in state["y", a, j]:
                c.wait_recv()
            s = ybuf[a, j, 0].astype(F32)
            for k in range(1, ny):
                s = s + ybuf[a, j, k].astype(F32)
            return s

        def stage3(a, j, finish):
            full[a, j, own, :] = finish(total(a, j), j).astype(BF16)
            state["ag", a, j] = remote(
                full.at[a, j, own, :], full.at[a, j, own, :], ag_s.at[a, j], ag_r.at[a, j], (g, mate)
            )

        def reduce_loop(a, product):
            for j in range(nc):
                stage1(a, j, product(j))
                if j >= 1:
                    stage2(a, j - 1)
            stage2(a, nc - 1)

        def gather_loop(a, finish, consume):
            for j in range(nc):
                stage3(a, j, finish)
                if j >= 1:
                    state["ag", a, j - 1].wait_recv()
                    consume(j - 1)
            state["ag", a, nc - 1].wait_recv()
            consume(nc - 1)

        reduce_loop(0, lambda j: mm(hidden[...], wdn[:, j * cw:(j + 1) * cw]))

        ir = lax.broadcasted_iota(jnp.int32, (tok, tok), 0)
        ic = lax.broadcasted_iota(jnp.int32, (tok, tok), 1)
        own_row = owner_ref[pl.ds(g, 1), :]
        own_bc = jnp.broadcast_to(own_row, (tok, tok))
        own_col = jnp.sum(jnp.where(ir == ic, own_bc, 0).astype(F32), axis=1, keepdims=True)
        before = ir < ic
        same = jnp.where((own_col == own_bc.astype(F32)) & before, 1.0, 0.0)
        rank_row = jnp.sum(same, axis=0, keepdims=True)
        place = own_row.astype(F32) * slots + rank_row
        srow = lax.broadcasted_iota(jnp.int32, (groups * slots, tok), 0).astype(F32)
        pick = jnp.where(srow == place, 1.0, 0.0).astype(BF16)
        outgoing[...] = mm(pick, teach_ref[...]).astype(BF16).reshape(groups, slots, fw)
        teach = []
        for k in range(1, groups):
            to = lax.rem(g + k, groups)
            teach.append(
                remote(outgoing.at[to], incoming.at[g], t_s.at[k - 1], t_r.at[k - 1], (to, t))
            )
        incoming[g] = outgoing[g]
        mine = owner_ref[...] == g
        tri = jnp.where(before, 1.0, 0.0).astype(BF16)
        rank = mm(jnp.where(mine, 1.0, 0.0).astype(BF16), tri)
        rank = jnp.where(mine, rank, -1.0)
        dest1 = slot_ref[...].astype(F32) + 1.0
        krow = lax.broadcasted_iota(jnp.int32, (slots, tok), 0).astype(F32)
        lane = lax.broadcasted_iota(jnp.int32, (slots, tok), 1).astype(F32)
        for s in range(groups):
            hit = jnp.where(krow == rank[s:s + 1, :], dest1[s:s + 1, :], 0.0)
            dest = jnp.sum(hit, axis=1, keepdims=True) - 1.0
            qt[s * slots:(s + 1) * slots, :] = jnp.where(lane == dest, 1.0, 0.0).astype(BF16)

        loads[2].wait()
        adapted[...] = jnp.zeros_like(adapted)

        def add_input(s, j):
            return s + x_ref[own, j * cw:(j + 1) * cw].astype(F32)

        def adapt(j):
            adapted[...] += mm(full[0, j], wad[j * cw:(j + 1) * cw, :])

        gather_loop(0, add_input, adapt)
        for c in teach:
            c.wait_recv()
        target = mm(qt[...], incoming[...].reshape(groups * slots, fw), TN)
        delta[...] = (adapted[...] - target).astype(BF16)

        reduce_loop(1, lambda j: mm(delta[...], wad[j * cw:(j + 1) * cw, :], NT))
        for j in range(nc):
            gp[j * cw:(j + 1) * cw, :] = mm(full[0, j], delta[...], TN)

        if reduce_groups:
            gx = lax.rem(g, 2)
            gz = lax.div(g, 2)

            def rows(xx, zz):
                return pl.ds(pl.multiple_of((xx * nz + zz) * blk, 16), blk)

            xmate = (gz * 2 + 1 - gx, t)
            xcopy, zcopy, azcopy, axcopy = {}, {}, {}, {}
            for k in list(range(1, nz)) + [0]:
                zz = lax.rem(gz + k, nz)
                xsend[k] = gp[rows(1 - gx, zz), :].astype(BF16)
                xcopy[k] = remote(xsend.at[k], xrecv.at[k], gx_s.at[k], gx_r.at[k], xmate)

            def z_step(k):
                xcopy[k].wait_recv()
                zz = lax.rem(gz + k, nz)
                zsend[k - 1] = (gp[rows(gx, zz), :] + xrecv[k].astype(F32)).astype(BF16)
                zcopy[k] = remote(
                    zsend.at[k - 1], zrecv.at[k - 1], gz_s.at[k - 1], gz_r.at[k - 1], (zz * 2 + gx, t)
                )

            def z_sum():
                xcopy[0].wait_recv()
                s = gp[rows(gx, gz), :] + xrecv[0].astype(F32)
                for k in range(1, nz):
                    zcopy[k].wait_recv()
                    s = s + zrecv[k - 1].astype(F32)
                b = gx * nz + gz
                gfull[b] = (s * scale).astype(BF16)
                for k in range(1, nz):
                    zz = lax.rem(gz + k, nz)
                    azcopy[k] = remote(
                        gfull.at[b], gfull.at[b], az_s.at[k - 1], az_r.at[k - 1], (zz * 2 + gx, t)
                    )
                axcopy[0] = remote(gfull.at[b], gfull.at[b], ax_s.at[0], ax_r.at[0], xmate)

            def z_gather(k):
                azcopy[k].wait_recv()
                b = gx * nz + lax.rem(gz - k + nz, nz)
                axcopy[k] = remote(gfull.at[b], gfull.at[b], ax_s.at[k], ax_r.at[k], xmate)
        else:
            ga_ref[...] = gp[...]

        gh[...] = jnp.zeros_like(gh)

        def back(j):
            gh[...] += mm(full[1, j], wdn[:, j * cw:(j + 1) * cw], NT)

        gather_loop(1, lambda s, j: s, back)
        gpre[...] = (gh[...] * dgelu[...]).astype(BF16)
        reduce_loop(2, lambda j: mm(gpre[...], wup[j * cw:(j + 1) * cw, :], NT))
        if reduce_groups:
            for k in range(1, nz):
                z_step(k)
        for j in range(nc):
            gtot[:, j * cw:(j + 1) * cw] = total(2, j)
        gn = gtot[...]
        xo = x_ref[own, :].astype(F32)
        cen = jnp.mean(xo, axis=-1, keepdims=True)
        dv = xo - cen
        r = lax.rsqrt(jnp.mean(jnp.square(dv), axis=-1, keepdims=True) + 1e-06)
        yn = dv * r
        gmean = jnp.mean(gn, axis=-1, keepdims=True)
        gy = jnp.mean(gn * yn, axis=-1, keepdims=True)
        dx = r * (gn - gmean - yn * gy)
        for j in range(nc):
            cs = slice(j * cw, (j + 1) * cw)
            oscr[own, cs] = (full[1, j, own, :].astype(F32) + dx[:, cs]).astype(BF16)
        ocopy = remote(oscr.at[own, :], oscr.at[own, :], o_s.at[0], o_r.at[0], (g, mate))
        if reduce_groups:
            z_sum()
        ocopy.wait_recv()
        ig_ref[...] = oscr[...]
        if reduce_groups:
            for k in range(1, nz):
                z_gather(k)
            for k in range(nz):
                axcopy[k].wait_recv()
            ga_ref[...] = gfull[...].astype(F32).reshape(d, fw)
        for c in sends:
            c.wait_send()

    vm = pltpu.VMEM
    dma = pltpu.SemaphoreType.DMA
    gb = (nz, blk, fw) if reduce_groups else (1, 16, 128)
    zb = (nz - 1, blk, fw) if reduce_groups else (1, 16, 128)
    fb = (groups, blk, fw) if reduce_groups else (1, 16, 128)
    nsem = nz if reduce_groups else 1
    scratch = [
        vm((d, ff), BF16), vm((ff, d), BF16), vm((d, fw), BF16), dma((3,)),
        vm((tok, d), BF16), vm((tok, ff), BF16), vm((tok, ff), F32),
        vm((2, nc, tok, cw), BF16), vm((3, nc, tok, cw), F32),
        vm((3, nc, half, cw), BF16), vm((3, nc, half, cw), BF16), vm((3, nc, ny, half, cw), BF16),
        dma((3, nc)), dma((3, nc)), dma((3, nc, ny - 1)), dma((3, nc, ny - 1)), dma((2, nc)), dma((2, nc)),
        vm((groups, slots, fw), BF16), vm((groups, slots, fw), BF16), vm((groups * slots, tok), BF16),
        dma((groups - 1,)), dma((groups - 1,)),
        vm((tok, fw), F32), vm((tok, fw), BF16), vm((tok, ff), F32), vm((tok, ff), BF16), vm((half, d), F32),
        vm((d, fw), F32), vm(gb, BF16), vm(gb, BF16), vm(zb, BF16), vm(zb, BF16), vm(fb, BF16),
        dma((nsem,)), dma((nsem,)), dma((nsem,)), dma((nsem,)),
        dma((nsem,)), dma((nsem,)), dma((nsem,)), dma((nsem,)),
        vm((tok, d), BF16), dma((1,)), dma((1,)),
    ]
    vspec = pl.BlockSpec(memory_space=pltpu.VMEM)
    aspec = pl.BlockSpec(memory_space=pl.ANY)
    return pl.pallas_call(
        kernel,
        out_shape=(jax.ShapeDtypeStruct((d, fw), F32), jax.ShapeDtypeStruct((tok, d), BF16)),
        in_specs=[vspec] * 5 + [aspec] * 3,
        out_specs=(vspec, vspec),
        scratch_shapes=scratch,
        compiler_params=pltpu.CompilerParams(
            collective_id=0, has_side_effects=True, vmem_limit_bytes=56 * 1024 * 1024
        ),
    )


def solution(mesh):
    groups = mesh.shape["group"]
    tensors = mesh.shape["tensor"]

    def per_device(student_in, teacher_feat, owner, slot_row, w_up, b_up, w_down, w_adapt):
        tok, d = student_in.shape
        fw = teacher_feat.shape[1]
        ff = w_up.shape[1]
        reduce_groups = groups % 2 == 0 and d % (groups * 16) == 0
        call = make_kernel(groups, tensors, tok, d, ff, fw, reduce_groups)
        grad_adapt, input_grad = call(
            student_in, teacher_feat, owner.reshape(groups, tok), slot_row.reshape(groups, tok),
            b_up.reshape(1, ff), w_up, w_down, w_adapt,
        )
        if not reduce_groups:
            grad_adapt = lax.psum(grad_adapt, "group") / math.sqrt(tok * groups)
        return grad_adapt, input_grad

    return jax.shard_map(
        per_device,
        mesh=mesh,
        in_specs=(
            P("group", None),
            P("group", "tensor"),
            P(),
            P(),
            P(None, "tensor"),
            P("tensor"),
            P("tensor", None),
            P(None, "tensor"),
        ),
        out_specs=(P(None, "tensor"), P("group", None)),
        check_vma=False,
    )
```

time: 246 us -> 71.9 us (0.29)
  waiting for transfers between devices: 158 us -> 0 us
  Pallas kernels: 0 us -> 62.5 us
  blocking collectives: 22.6 us -> 0 us
  matrix products: 17.4 us -> 0 us
  between operations: 13.9 us -> 0.65 us
  other arithmetic: 10.4 us -> 0 us
  local copies, waits for them, and re-layouts: 15.5 us -> 7.8 us
  starting transfers between devices: 7.35 us -> 0 us
    psum x3 -> x0, waiting for transfers between devices: 158 us -> none  [the longest x1 97.1 us: per_device(): grad_adapt = lax.psum(grad_part, 'group')]
    pallas_call x0 -> x1, Pallas kernels: none -> 62.5 us  [per_device(): call(student_in, teacher_feat, owner.reshape(groups, tok), slot_row.resha...]
    psum x1 -> x0, blocking collectives: 22.6 us -> none  [tensor_total(): summed = lax.psum(partial_value, 'tensor')]
    dot_general x6 -> x0, matrix products: 17.4 us -> none  [the longest x1 5.85 us: per_device(): jnp.dot(grad_pre, w_up.T, preferred_element_type=jnp.float32)]
    scatter x2 -> x0, local copies, waits for them, and re-layouts: 8.42 us -> none  [the longest x1 6.18 us: per_device(): jnp.zeros((tok_rows,), jnp.int32).at[dest_index]]
    all_to_all x1 -> x0, starting transfers between devices: 7.23 us -> none  [per_device(): lax.all_to_all(outgoing.reshape(groups, slot_count, feat_width), 'group',...]
    reduce_sum x5 -> x0, other arithmetic: 5.49 us -> none  [the longest x2 2.62 us: normalize(): spread = jnp.mean(jnp.square(values - center), axis=-1, keepdims=True)]
    reshape x1 -> x3, local copies, waits for them, and re-layouts: 0.08 us -> 4.02 us  [the longest x1 1.36 us: per_device(): slot_row.reshape(groups, tok)]
  transfers between devices with their start and end apart: 4 -> 0, of which waited for: 3 -> 0; matrix products, arithmetic and copies ran while one was open for 10% -> 0% of each run, Pallas kernels for 0% -> 0%
where the time goes in v1:
time: 71.9 us; the launch traced here: 71 us
  Pallas kernels  62.5 us (87%)
  local copies, waits for them, and re-layouts  7.8 us (11%)
    pallas_call x1, Pallas kernels, per_device(): call(student_in, teacher_feat, owner.reshape(groups, tok), slot_row.resha...  62.5 us
    unnamed x4, local copies, waits for them, and re-layouts  3.78 us

profile of v1, /device:TPU:0, one launch (start us, length us, event | category | flops | bytes accessed | tf_op | source)
XLA Modules:
  0.0 71.0 jit_solution(10484608421631741562)
XLA Ops:
  0.6 1.3 %reshape.15.b_ref = f32[1,1280]{1,0:T(1,128)} reshape(f32[1280]{0:T(1024)} %param.13) | data formatting | bytes 10240 | tf_op jit(solution)/shard_map/reshape | solution.py:329
  1.9 1.4 %reshape.13.owner_ref = s32[8,192]{1,0:T(8,128)} reshape(s32[1536]{0:T(1024)} %param.10) | data formatting | bytes 12288 | tf_op jit(solution)/shard_map/reshape | solution.py:328
  3.3 1.4 %reshape.14.slot_ref = s32[8,192]{1,0:T(8,128)} reshape(s32[1536]{0:T(1024)} %param.11) | data formatting | bytes 12288 | tf_op jit(solution)/shard_map/reshape | solution.py:328
  4.7 62.5 %shard_map.95 = (f32[1280,384]{1,0:T(8,128)}, bf16[192,1280]{1,0:T(8,128)(2,1)}) custom-call(bf16[192,1280]{1,0:T(8,128)(2,1)} %x_ref.1, bf16[192,384]{1,0:T(8,128)(2,1)} %teach_ref.1, s32[8,192]{1,0:T(8,128)} %reshape.13.owner_ref, s32[8,192]{1,0:T(8,128)} %reshape.14.slot_ref, f32[1,1280]{1,0:T(1,128)} %reshape.15.b_ref, bf16[1280,1280]{1,0:T(8,128)(2,1)} %wup_hbm.1, ...), custom_call_target="tpu_custom_call" | custom-call | tf_op jit(solution)/shard_map/pallas_call | solution.py:327
  67.2 0.0 copy-start
  67.2 3.0 %copy.12 = f32[1280,384]{1,0:T(8,128)} copy(f32[1280,384]{1,0:T(8,128)} %get-tuple-element.4) | data formatting | bytes 3932160
  70.2 0.0 copy-done
  70.2 0.8 %copy.13 = bf16[192,1280]{1,0:T(8,128)(2,1)} copy(bf16[192,1280]{1,0:T(8,128)(2,1)S(1)} %copy-done) | data formatting | bytes 983040
Async XLA Ops:
  67.2 3.0 %copy-start = (bf16[192,1280]{1,0:T(8,128)(2,1)S(1)}, bf16[192,1280]{1,0:T(8,128)(2,1)}, u32[]{:S(2)}) copy-start(bf16[192,1280]{1,0:T(8,128)(2,1)} %get-tuple-element.5) | copy-start | bytes 1474564

commit v2 on v1

--- a/solution.py
+++ b/solution.py
@@ -26,6 +26,7 @@
     ny = tensors // 2
     half = tok // 2
     cw = 256
+    hw = cw // 2
     uw = math.gcd(ff, 256)
     nc = d // cw
     slots = RUN * ((tok // RUN + groups - 1) // groups)
@@ -35,15 +36,15 @@
     scale = 1.0 / math.sqrt(tok * groups)
 
     def kernel(
-        x_ref, teach_ref, owner_ref, slot_ref, b_ref, wup_hbm, wdn_hbm, wad_hbm,
+        x_ref, teach_ref, owner_in, slot_in, b_ref, wup_hbm, wdn_hbm, wad_hbm,
         ga_ref, ig_ref,
         wup, wdn, wad, wsem,
         normed, hidden, dgelu, full, part, send1, recv1, ybuf,
         s1_s, s1_r, y_s, y_r, ag_s, ag_r,
         outgoing, incoming, qt, t_s, t_r,
         adapted, delta, gh, gpre, gtot,
-        gp, xsend, xrecv, zsend, zrecv, gfull, gx_s, gx_r, gz_s, gz_r, az_s, az_r, ax_s, ax_r,
-        oscr, o_s, o_r,
+        so_mate, d_mate, gsum, zsend, zrecv, gfull, so_s, so_r, d_s, d_r, gz_s, gz_r, az_s, az_r, ax_s, ax_r,
+        oscr, o_s, o_r, owner_ref, slot_ref,
     ):
         g = lax.axis_index("group")
         t = lax.axis_index("tensor")
@@ -86,7 +87,7 @@
         loads[0].wait()
         for j in range(ff // uw):
             cs = slice(j * uw, (j + 1) * uw)
-            pre = mm(normed[...], wup[:, cs]) + b_ref[:, cs]
+            pre = mm(normed[...], wup[:, cs]) + b_ref[cs][None, :]
             sq = pre * pre
             th = jnp.tanh(GELU_K * pre * (1.0 + GELU_A * sq))
             hidden[:, cs] = (0.5 * pre * (1.0 + th)).astype(BF16)
@@ -147,6 +148,9 @@
 
         reduce_loop(0, lambda j: mm(hidden[...], wdn[:, j * cw:(j + 1) * cw]))
 
+        for s in range(groups):
+            owner_ref[s:s + 1, :] = owner_in[s * tok:(s + 1) * tok][None, :]
+            slot_ref[s:s + 1, :] = slot_in[s * tok:(s + 1) * tok][None, :]
         ir = lax.broadcasted_iota(jnp.int32, (tok, tok), 0)
         ic = lax.broadcasted_iota(jnp.int32, (tok, tok), 1)
         own_row = owner_ref[pl.ds(g, 1), :]
@@ -184,7 +188,15 @@
         def add_input(s, j):
             return s + x_ref[own, j * cw:(j + 1) * cw].astype(F32)
 
+        gx = lax.rem(g, 2)
+        gz = lax.div(g, 2)
+        xmate = (gz * 2 + 1 - gx, t)
+        lane0 = pl.ds(pl.multiple_of(gx * hw, hw), hw)
+        lane1 = pl.ds(pl.multiple_of((1 - gx) * hw, hw), hw)
+
         def adapt(j):
+            if reduce_groups:
+                state["so", j] = remote(full.at[0, j, :, lane1], so_mate.at[j], so_s.at[j], so_r.at[j], xmate)
             adapted[...] += mm(full[0, j], wad[j * cw:(j + 1) * cw, :])
 
         gather_loop(0, add_input, adapt)
@@ -193,53 +205,51 @@
         target = mm(qt[...], incoming[...].reshape(groups * slots, fw), TN)
         delta[...] = (adapted[...] - target).astype(BF16)
 
+        if reduce_groups:
+            dcopy = remote(delta, d_mate, d_s.at[0], d_r.at[0], xmate)
+
         reduce_loop(1, lambda j: mm(delta[...], wad[j * cw:(j + 1) * cw, :], NT))
-        for j in range(nc):
-            gp[j * cw:(j + 1) * cw, :] = mm(full[0, j], delta[...], TN)
-
-        if reduce_groups:
-            gx = lax.rem(g, 2)
-            gz = lax.div(g, 2)
-
-            def rows(xx, zz):
-                return pl.ds(pl.multiple_of((xx * nz + zz) * blk, 16), blk)
-
-            xmate = (gz * 2 + 1 - gx, t)
-            xcopy, zcopy, azcopy, axcopy = {}, {}, {}, {}
-            for k in list(range(1, nz)) + [0]:
+
+        zcopy, azcopy, axcopy = {}, {}, {}
+
+        def rows(zz):
+            return pl.ds(pl.multiple_of(zz * blk, 16), blk)
+
+        def z_send():
+            dcopy.wait_recv()
+            for j in range(nc):
+                state["so", j].wait_recv()
+                v = mm(full[0, j, :, lane0], delta[...], TN) + mm(so_mate[j], d_mate[...], TN)
+                gsum[j * hw:(j + 1) * hw, :] = v
+                zsend[j * hw:(j + 1) * hw, :] = v.astype(BF16)
+            for k in range(1, nz):
                 zz = lax.rem(gz + k, nz)
-                xsend[k] = gp[rows(1 - gx, zz), :].astype(BF16)
-                xcopy[k] = remote(xsend.at[k], xrecv.at[k], gx_s.at[k], gx_r.at[k], xmate)
-
-            def z_step(k):
-                xcopy[k].wait_recv()
+                zcopy[k] = remote(
+                    zsend.at[rows(zz), :], zrecv.at[k - 1], gz_s.at[k - 1], gz_r.at[k - 1], (zz * 2 + gx, t)
+                )
+
+        def z_sum():
+            s = gsum[rows(gz), :]
+            for k in range(1, nz):
+                zcopy[k].wait_recv()
+                s = s + zrecv[k - 1].astype(F32)
+            gfull[gx, rows(gz), :] = (s * scale).astype(BF16)
+            blkref = gfull.at[gx, rows(gz), :]
+            for k in range(1, nz):
                 zz = lax.rem(gz + k, nz)
-                zsend[k - 1] = (gp[rows(gx, zz), :] + xrecv[k].astype(F32)).astype(BF16)
-                zcopy[k] = remote(
-                    zsend.at[k - 1], zrecv.at[k - 1], gz_s.at[k - 1], gz_r.at[k - 1], (zz * 2 + gx, t)
-                )
-
-            def z_sum():
-                xcopy[0].wait_recv()
-                s = gp[rows(gx, gz), :] + xrecv[0].astype(F32)
-                for k in range(1, nz):
-                    zcopy[k].wait_recv()
-                    s = s + zrecv[k - 1].astype(F32)
-                b = gx * nz + gz
-                gfull[b] = (s * scale).astype(BF16)
-                for k in range(1, nz):
-                    zz = lax.rem(gz + k, nz)
-                    azcopy[k] = remote(
-                        gfull.at[b], gfull.at[b], az_s.at[k - 1], az_r.at[k - 1], (zz * 2 + gx, t)
-                    )
-                axcopy[0] = remote(gfull.at[b], gfull.at[b], ax_s.at[0], ax_r.at[0], xmate)
-
-            def z_gather(k):
-                azcopy[k].wait_recv()
-                b = gx * nz + lax.rem(gz - k + nz, nz)
-                axcopy[k] = remote(gfull.at[b], gfull.at[b], ax_s.at[k], ax_r.at[k], xmate)
+                azcopy[k] = remote(blkref, blkref, az_s.at[k - 1], az_r.at[k - 1], (zz * 2 + gx, t))
+            axcopy[0] = remote(blkref, blkref, ax_s.at[0], ax_r.at[0], xmate)
+
+        def z_gather(k):
+            azcopy[k].wait_recv()
+            blkref = gfull.at[gx, rows(lax.rem(gz - k + nz, nz)), :]
+            axcopy[k] = remote(blkref, blkref, ax_s.at[k], ax_r.at[k], xmate)
+
+        if reduce_groups:
+            z_send()
         else:
-            ga_ref[...] = gp[...]
+            for j in range(nc):
+                ga_ref[j * cw:(j + 1) * cw, :] = mm(full[0, j], delta[...], TN)
 
         gh[...] = jnp.zeros_like(gh)
 
@@ -250,10 +260,11 @@
         gpre[...] = (gh[...] * dgelu[...]).astype(BF16)
         reduce_loop(2, lambda j: mm(gpre[...], wup[j * cw:(j + 1) * cw, :], NT))
         if reduce_groups:
-            for k in range(1, nz):
-                z_step(k)
+            z_sum()
         for j in range(nc):
             gtot[:, j * cw:(j + 1) * cw] = total(2, j)
+        if reduce_groups:
+            z_gather(1)
         gn = gtot[...]
         xo = x_ref[own, :].astype(F32)
         cen = jnp.mean(xo, axis=-1, keepdims=True)
@@ -268,23 +279,27 @@
             oscr[own, cs] = (full[1, j, own, :].astype(F32) + dx[:, cs]).astype(BF16)
         ocopy = remote(oscr.at[own, :], oscr.at[own, :], o_s.at[0], o_r.at[0], (g, mate))
         if reduce_groups:
-            z_sum()
+            for k in range(2, nz):
+                z_gather(k)
         ocopy.wait_recv()
         ig_ref[...] = oscr[...]
         if reduce_groups:
-            for k in range(1, nz):
-                z_gather(k)
             for k in range(nz):
                 axcopy[k].wait_recv()
-            ga_ref[...] = gfull[...].astype(F32).reshape(d, fw)
+            for j in range(nc):
+                for xx in range(2):
+                    r0 = j * cw + xx * hw
+                    ga_ref[r0:r0 + hw, :] = gfull[xx, j * hw:(j + 1) * hw, :]
         for c in sends:
             c.wait_send()
 
     vm = pltpu.VMEM
     dma = pltpu.SemaphoreType.DMA
-    gb = (nz, blk, fw) if reduce_groups else (1, 16, 128)
+    gb = (d // 2, fw) if reduce_groups else (16, 128)
     zb = (nz - 1, blk, fw) if reduce_groups else (1, 16, 128)
-    fb = (groups, blk, fw) if reduce_groups else (1, 16, 128)
+    fb = (2, d // 2, fw) if reduce_groups else (1, 16, 128)
+    mb = (nc, tok, hw) if reduce_groups else (1, 16, 128)
+    db = (tok, fw) if reduce_groups else (16, 128)
     nsem = nz if reduce_groups else 1
     scratch = [
         vm((d, ff), BF16), vm((ff, d), BF16), vm((d, fw), BF16), dma((3,)),
@@ -295,16 +310,16 @@
         vm((groups, slots, fw), BF16), vm((groups, slots, fw), BF16), vm((groups * slots, tok), BF16),
         dma((groups - 1,)), dma((groups - 1,)),
         vm((tok, fw), F32), vm((tok, fw), BF16), vm((tok, ff), F32), vm((tok, ff), BF16), vm((half, d), F32),
-        vm((d, fw), F32), vm(gb, BF16), vm(gb, BF16), vm(zb, BF16), vm(zb, BF16), vm(fb, BF16),
+        vm(mb, BF16), vm(db, BF16), vm(gb, F32), vm(gb, BF16), vm(zb, BF16), vm(fb, BF16),
+        dma((nc,)), dma((nc,)), dma((1,)), dma((1,)), dma((nsem,)), dma((nsem,)),
         dma((nsem,)), dma((nsem,)), dma((nsem,)), dma((nsem,)),
-        dma((nsem,)), dma((nsem,)), dma((nsem,)), dma((nsem,)),
-        vm((tok, d), BF16), dma((1,)), dma((1,)),
+        vm((tok, d), BF16), dma((1,)), dma((1,)), vm((groups, tok), jnp.int32), vm((groups, tok), jnp.int32),
     ]
     vspec = pl.BlockSpec(memory_space=pltpu.VMEM)
     aspec = pl.BlockSpec(memory_space=pl.ANY)
     return pl.pallas_call(
         kernel,
-        out_shape=(jax.ShapeDtypeStruct((d, fw), F32), jax.ShapeDtypeStruct((tok, d), BF16)),
+        out_shape=(jax.ShapeDtypeStruct((d, fw), BF16 if reduce_groups else F32), jax.ShapeDtypeStruct((tok, d), BF16)),
         in_specs=[vspec] * 5 + [aspec] * 3,
         out_specs=(vspec, vspec),
         scratch_shapes=scratch,
@@ -325,10 +340,11 @@
         reduce_groups = groups % 2 == 0 and d % (groups * 16) == 0
         call = make_kernel(groups, tensors, tok, d, ff, fw, reduce_groups)
         grad_adapt, input_grad = call(
-            student_in, teacher_feat, owner.reshape(groups, tok), slot_row.reshape(groups, tok),
-            b_up.reshape(1, ff), w_up, w_down, w_adapt,
+            student_in, teacher_feat, owner, slot_row, b_up, w_up, w_down, w_adapt,
         )
-        if not reduce_groups:
+        if reduce_groups:
+            grad_adapt = grad_adapt.astype(F32)
+        else:
             grad_adapt = lax.psum(grad_adapt, "group") / math.sqrt(tok * groups)
         return grad_adapt, input_grad
 

time: 71.9 us -> 60.1 us (0.84)
  Pallas kernels: 62.5 us -> 55.3 us
  local copies, waits for them, and re-layouts: 7.8 us -> 0.78 us
  other arithmetic: 0 us -> 2.66 us
    pallas_call x1, Pallas kernels: 62.5 us -> 55.3 us  [per_device(): call(student_in, teacher_feat, owner, slot_row, b_up, w_up, w_down, w_adapt)]
    reshape x3 -> x0, local copies, waits for them, and re-layouts: 4.02 us -> none  [the longest x1 1.36 us: per_device(): slot_row.reshape(groups, tok)]
    unnamed x4 -> x3, local copies, waits for them, and re-layouts: 3.78 us -> 0.78 us
    convert_element_type x0 -> x1, other arithmetic: none -> 2.66 us  [per_device(): grad_adapt = grad_adapt.astype(F32)]
where the time goes in v2:
time: 60.1 us; the launch traced here: 59.4 us
  Pallas kernels  55.3 us (92%)
  other arithmetic  2.66 us (4%)
  local copies, waits for them, and re-layouts  0.78 us (1%)
  between operations  0.65 us (1%)
    pallas_call x1, Pallas kernels, per_device(): call(student_in, teacher_feat, owner, slot_row, b_up, w_up, w_down, w_adapt)  55.3 us
    convert_element_type x1, other arithmetic, per_device(): grad_adapt = grad_adapt.astype(F32)  2.66 us

profile of v2, /device:TPU:0, one launch (start us, length us, event | category | flops | bytes accessed | tf_op | source)
XLA Modules:
  0.0 59.4 jit_solution(8661515333012490436)
XLA Ops:
  0.6 55.3 %shard_map.95 = (bf16[1280,384]{1,0:T(8,128)(2,1)}, bf16[192,1280]{1,0:T(8,128)(2,1)}) custom-call(bf16[192,1280]{1,0:T(8,128)(2,1)} %x_ref.1, bf16[192,384]{1,0:T(8,128)(2,1)} %teach_ref.1, s32[1536]{0:T(1024)} %owner_in.1, s32[1536]{0:T(1024)} %slot_in.1, f32[1280]{0:T(1024)} %b_ref.1, bf16[1280,1280]{1,0:T(8,128)(2,1)} %wup_hbm.1, ...), custom_call_target="tpu_custom_call" | custom-call | tf_op jit(solution)/shard_map/pallas_call | solution.py:342
  56.0 0.0 copy-start
  56.0 2.7 %convert_element_type.3 = f32[1280,384]{1,0:T(8,128)} convert(bf16[1280,384]{1,0:T(8,128)(2,1)} %get-tuple-element.4) | non-fusion elementwise | flops 491520 | bytes 2949120 | tf_op jit(solution)/shard_map/convert_element_type | solution.py:346
  58.6 0.0 copy-done
  58.6 0.8 %copy.11 = bf16[192,1280]{1,0:T(8,128)(2,1)} copy(bf16[192,1280]{1,0:T(8,128)(2,1)S(1)} %copy-done) | data formatting | bytes 983040
Async XLA Ops:
  56.0 2.7 %copy-start = (bf16[192,1280]{1,0:T(8,128)(2,1)S(1)}, bf16[192,1280]{1,0:T(8,128)(2,1)}, u32[]{:S(2)}) copy-start(bf16[192,1280]{1,0:T(8,128)(2,1)} %get-tuple-element.9) | copy-start | bytes 1474564

commit v3 on v2

v3 whole, which is shorter than its diff:
```python
import math

import jax
import jax.numpy as jnp
from jax import lax
from jax.experimental import pallas as pl
from jax.experimental.pallas import tpu as pltpu
from jax.sharding import PartitionSpec as P

RUN = 2
MESH = pl.DeviceIdType.MESH
F32 = jnp.float32
BF16 = jnp.bfloat16
NN = (((1,), (0,)), ((), ()))
NT = (((1,), (1,)), ((), ()))
TN = (((0,), (0,)), ((), ()))
GELU_K = math.sqrt(2.0 / math.pi)
GELU_A = 0.044715


def mm(a, b, dims=NN):
    return lax.dot_general(a, b, dims, preferred_element_type=F32)


def make_kernel(groups, tensors, tok, d, ff, fw, reduce_groups):
    ny = tensors // 2
    half = tok // 2
    cw = 256
    hw = cw // 2
    uw = math.gcd(ff, 256)
    nc = d // cw
    slots = RUN * ((tok // RUN + groups - 1) // groups)
    slots = 16 * ((slots + 15) // 16)
    nz = groups // 2
    nch = fw // 128 if reduce_groups else 1
    blk = d // groups if reduce_groups else 8
    scale = 1.0 / math.sqrt(tok * groups)

    def kernel(
        x_ref, teach_ref, owner_in, slot_in, b_ref, wup_hbm, wdn_hbm, wad_hbm,
        ga_ref, ig_ref,
        wup, wdn, wad, wsem,
        normed, hidden, dgelu, full, part, send1, recv1, ybuf,
        s1_s, s1_r, y_s, y_r, ag_s, ag_r,
        outgoing, incoming, qt, t_s, t_r,
        adapted, delta, gh, gpre, gtot,
        so_mate, d_mate, gsum, zsend, zrecv, gfull, so_s, so_r, d_s, d_r, gz_s, gz_r, az_s, az_r, ax_s, ax_r,
        oscr, o_s, o_r, owner_ref, slot_ref, out_s,
    ):
        g = lax.axis_index("group")
        t = lax.axis_index("tensor")
        core = lax.rem(t, 2)
        y = lax.div(t, 2)
        mate = t + 1 - 2 * core
        own0 = pl.multiple_of(core * half, 16)
        oth0 = pl.multiple_of((1 - core) * half, 16)
        own = pl.ds(own0, half)
        oth = pl.ds(oth0, half)

        gx = lax.rem(g, 2)
        gz = lax.div(g, 2)
        xmate = (gz * 2 + 1 - gx, t)
        def cols(c):
            return slice(c * 128, (c + 1) * 128)

        lane0 = pl.ds(pl.multiple_of(gx * hw, hw), hw)
        lane1 = pl.ds(pl.multiple_of((1 - gx) * hw, hw), hw)

        barrier = pltpu.get_barrier_semaphore()
        for k in range(1, tensors):
            pl.semaphore_signal(barrier, inc=1, device_id=(g, lax.rem(t + k, tensors)), device_id_type=MESH)
        for k in range(1, groups):
            pl.semaphore_signal(barrier, inc=1, device_id=(lax.rem(g + k, groups), t), device_id_type=MESH)

        loads = [
            pltpu.make_async_copy(src, dst, wsem.at[i])
            for i, (src, dst) in enumerate(((wup_hbm, wup), (wdn_hbm, wdn), (wad_hbm, wad)))
        ]
        for c in loads:
            c.start()

        sends = []

        def remote(src, dst, ss, rs, dev):
            c = pltpu.make_async_remote_copy(
                src_ref=src, dst_ref=dst, send_sem=ss, recv_sem=rs, device_id=dev, device_id_type=MESH
            )
            c.start()
            sends.append(c)
            return c

        xf = x_ref[...].astype(F32)
        cen = jnp.mean(xf, axis=-1, keepdims=True)
        dev_ = xf - cen
        rstd = lax.rsqrt(jnp.mean(jnp.square(dev_), axis=-1, keepdims=True) + 1e-06)
        normed[...] = (dev_ * rstd).astype(BF16)
        for s in range(groups):
            owner_ref[s:s + 1, :] = owner_in[s * tok:(s + 1) * tok][None, :]
            slot_ref[s:s + 1, :] = slot_in[s * tok:(s + 1) * tok][None, :]
        ir = lax.broadcasted_iota(jnp.int32, (tok, tok), 0)
        ic = lax.broadcasted_iota(jnp.int32, (tok, tok), 1)
        own_row = owner_ref[pl.ds(g, 1), :]
        own_bc = jnp.broadcast_to(own_row, (tok, tok))
        own_col = jnp.sum(jnp.where(ir == ic, own_bc, 0).astype(F32), axis=1, keepdims=True)
        before = ir < ic
        same = jnp.where((own_col == own_bc.astype(F32)) & before, 1.0, 0.0)
        rank_row = jnp.sum(same, axis=0, keepdims=True)
        place = own_row.astype(F32) * slots + rank_row
        srow = lax.broadcasted_iota(jnp.int32, (groups * slots, tok), 0).astype(F32)
        pick = jnp.where(srow == place, 1.0, 0.0).astype(BF16)
        outgoing[...] = mm(pick, teach_ref[...]).astype(BF16).reshape(groups, slots, fw)
        pl.semaphore_wait(barrier, tensors - 1 + groups - 1)
        teach = []
        for k in range(1, groups):
            to = lax.rem(g + k, groups)
            teach.append(
                remote(outgoing.at[to], incoming.at[g], t_s.at[k - 1], t_r.at[k - 1], (to, t))
            )
        incoming[g] = outgoing[g]
        loads[0].wait()
        for j in range(ff // uw):
            cs = slice(j * uw, (j + 1) * uw)
            pre = mm(normed[...], wup[:, cs]) + b_ref[cs][None, :]
            sq = pre * pre
            th = jnp.tanh(GELU_K * pre * (1.0 + GELU_A * sq))
            hidden[:, cs] = (0.5 * pre * (1.0 + th)).astype(BF16)
            dgelu[:, cs] = 0.5 * (1.0 + th) + 0.5 * GELU_K * pre * (1.0 - th * th) * (1.0 + 3.0 * GELU_A * sq)

        loads[1].wait()

        state = {}

        def stage1(a, j, value):
            part[a, j] = value
            send1[a, j] = part[a, j, oth, :].astype(BF16)
            state["s1", a, j] = remote(
                send1.at[a, j], recv1.at[a, j], s1_s.at[a, j], s1_r.at[a, j], (g, mate)
            )

        def stage2(a, j):
            state["s1", a, j].wait_recv()
            ybuf[a, j, y] = (part[a, j, own, :] + recv1[a, j].astype(F32)).astype(BF16)
            state["y", a, j] = [
                remote(
                    ybuf.at[a, j, y], ybuf.at[a, j, y], y_s.at[a, j, k - 1], y_r.at[a, j, k - 1],
                    (g, lax.rem(y + k, ny) * 2 + core),
                )
                for k in range(1, ny)
            ]

        def total(a, j):
            for c in state["y", a, j]:
                c.wait_recv()
            s = ybuf[a, j, 0].astype(F32)
            for k in range(1, ny):
                s = s + ybuf[a, j, k].astype(F32)
            return s

        def stage3(a, j, finish):
            full[a, j, own, :] = finish(total(a, j), j).astype(BF16)
            state["ag", a, j] = remote(
                full.at[a, j, own, :], full.at[a, j, own, :], ag_s.at[a, j], ag_r.at[a, j], (g, mate)
            )
            if a == 0 and reduce_groups:
                state["so", j] = remote(
                    full.at[0, j, own, lane1], so_mate.at[j, own, :], so_s.at[0, j], so_r.at[0, j], xmate
                )

        def reduce_loop(a, product):
            for j in range(nc):
                stage1(a, j, product(j))
                if j >= 1:
                    stage2(a, j - 1)
            stage2(a, nc - 1)

        def gather_loop(a, finish, consume):
            for j in range(nc):
                stage3(a, j, finish)
                if j >= 1:
                    state["ag", a, j - 1].wait_recv()
                    consume(j - 1)
            state["ag", a, nc - 1].wait_recv()
            consume(nc - 1)

        reduce_loop(0, lambda j: mm(hidden[...], wdn[:, j * cw:(j + 1) * cw]))

        mine = owner_ref[...] == g
        tri = jnp.where(before, 1.0, 0.0).astype(BF16)
        rank = mm(jnp.where(mine, 1.0, 0.0).astype(BF16), tri)
        rank = jnp.where(mine, rank, -1.0)
        dest1 = slot_ref[...].astype(F32) + 1.0
        krow = lax.broadcasted_iota(jnp.int32, (slots, tok), 0).astype(F32)
        lane = lax.broadcasted_iota(jnp.int32, (slots, tok), 1).astype(F32)
        for s in range(groups):
            hit = jnp.where(krow == rank[s:s + 1, :], dest1[s:s + 1, :], 0.0)
            dest = jnp.sum(hit, axis=1, keepdims=True) - 1.0
            qt[s * slots:(s + 1) * slots, :] = jnp.where(lane == dest, 1.0, 0.0).astype(BF16)

        loads[2].wait()
        adapted[...] = jnp.zeros_like(adapted)

        def add_input(s, j):
            return s + x_ref[own, j * cw:(j + 1) * cw].astype(F32)

        def adapt(j):
            adapted[...] += mm(full[0, j], wad[j * cw:(j + 1) * cw, :])

        gather_loop(0, add_input, adapt)
        for c in teach:
            c.wait_recv()
        target = mm(qt[...], incoming[...].reshape(groups * slots, fw), TN)
        delta[...] = (adapted[...] - target).astype(BF16)

        if reduce_groups:
            dcopy = [
                remote(delta.at[:, cols(c)], d_mate.at[:, cols(c)], d_s.at[c], d_r.at[c], xmate) for c in range(nch)
            ]

        reduce_loop(1, lambda j: mm(delta[...], wad[j * cw:(j + 1) * cw, :], NT))

        zcopy, azcopy, axcopy = {}, {}, {}

        def rows(zz):
            return pl.ds(pl.multiple_of(zz * blk, 16), blk)

        def z_send():
            for j in range(nc):
                state["so", j].wait_recv()
                state["so2", j] = remote(
                    so_mate.at[j, own, :], so_mate.at[j, own, :], so_s.at[1, j], so_r.at[1, j], (g, mate)
                )
            for j in range(nc):
                v = mm(full[0, j, :, lane0], delta[...], TN)
                for c in range(nch):
                    gsum[c, j * hw:(j + 1) * hw, :] = v[:, cols(c)]
            for c in range(nch):
                dcopy[c].wait_recv()
            for j in range(nc):
                state["so2", j].wait_recv()
                v = mm(so_mate[j], d_mate[...], TN)
                for c in range(nch):
                    w = gsum[c, j * hw:(j + 1) * hw, :] + v[:, cols(c)]
                    gsum[c, j * hw:(j + 1) * hw, :] = w
                    zsend[c, j * hw:(j + 1) * hw, :] = w.astype(BF16)
            for c in range(nch):
                for k in range(1, nz):
                    zz = lax.rem(gz + k, nz)
                    zcopy[c, k] = remote(
                        zsend.at[c, rows(zz), :], zrecv.at[c, k - 1], gz_s.at[c, k - 1], gz_r.at[c, k - 1],
                        (zz * 2 + gx, t),
                    )

        def z_sum(c):
            s = gsum[c, rows(gz), :]
            for k in range(1, nz):
                zcopy[c, k].wait_recv()
                s = s + zrecv[c, k - 1].astype(F32)
            gfull[c, gx, rows(gz), :] = (s * scale).astype(BF16)
            blkref = gfull.at[c, gx, rows(gz), :]
            for k in range(1, nz):
                zz = lax.rem(gz + k, nz)
                azcopy[c, k] = remote(blkref, blkref, az_s.at[c, k - 1], az_r.at[c, k - 1], (zz * 2 + gx, t))
            axcopy[c, 0] = remote(blkref, blkref, ax_s.at[c, 0], ax_r.at[c, 0], xmate)

        def z_gather(c):
            for k in range(1, nz):
                azcopy[c, k].wait_recv()
                blkref = gfull.at[c, gx, rows(lax.rem(gz - k + nz, nz)), :]
                axcopy[c, k] = remote(blkref, blkref, ax_s.at[c, k], ax_r.at[c, k], xmate)

        if reduce_groups:
            z_send()
        else:
            for j in range(nc):
                ga_ref[j * cw:(j + 1) * cw, :] = mm(full[0, j], delta[...], TN)

        gh[...] = jnp.zeros_like(gh)

        def back(j):
            gh[...] += mm(full[1, j], wdn[:, j * cw:(j + 1) * cw], NT)

        gather_loop(1, lambda s, j: s, back)
        gpre[...] = (gh[...] * dgelu[...]).astype(BF16)
        if reduce_groups:
            z_sum(0)
        reduce_loop(2, lambda j: mm(gpre[...], wup[j * cw:(j + 1) * cw, :], NT))
        if reduce_groups:
            for c in range(1, nch):
                z_sum(c)
        for j in range(nc):
            gtot[:, j * cw:(j + 1) * cw] = total(2, j)
        gn = gtot[...]
        xo = x_ref[own, :].astype(F32)
        cen = jnp.mean(xo, axis=-1, keepdims=True)
        dv = xo - cen
        r = lax.rsqrt(jnp.mean(jnp.square(dv), axis=-1, keepdims=True) + 1e-06)
        yn = dv * r
        gmean = jnp.mean(gn, axis=-1, keepdims=True)
        gy = jnp.mean(gn * yn, axis=-1, keepdims=True)
        dx = r * (gn - gmean - yn * gy)
        for j in range(nc):
            cs = slice(j * cw, (j + 1) * cw)
            oscr[own, cs] = (full[1, j, own, :].astype(F32) + dx[:, cs]).astype(BF16)
        ocopy = remote(oscr.at[own, :], oscr.at[own, :], o_s.at[0], o_r.at[0], (g, mate))
        if reduce_groups:
            for c in range(nch):
                z_gather(c)
        ocopy.wait_recv()
        outs = [pltpu.make_async_copy(oscr, ig_ref, out_s.at[nch])]
        outs[0].start()
        if reduce_groups:
            for c in range(nch):
                for k in range(nz):
                    axcopy[c, k].wait_recv()
                outs.append(pltpu.make_async_copy(gfull.at[c], ga_ref.at[c], out_s.at[c]))
                outs[-1].start()
        for c in outs:
            c.wait()
        for c in sends:
            c.wait_send()

    vm = pltpu.VMEM
    dma = pltpu.SemaphoreType.DMA
    gb = (nch, d // 2, 128) if reduce_groups else (1, 16, 128)
    zb = (nch, nz - 1, blk, 128) if reduce_groups else (1, 1, 16, 128)
    fb = (nch, 2, d // 2, 128) if reduce_groups else (1, 1, 16, 128)
    mb = (nc, tok, hw) if reduce_groups else (1, 16, 128)
    db = (tok, fw) if reduce_groups else (16, 128)
    nsem = nz if reduce_groups else 1
    scratch = [
        vm((d, ff), BF16), vm((ff, d), BF16), vm((d, fw), BF16), dma((3,)),
        vm((tok, d), BF16), vm((tok, ff), BF16), vm((tok, ff), F32),
        vm((2, nc, tok, cw), BF16), vm((3, nc, tok, cw), F32),
        vm((3, nc, half, cw), BF16), vm((3, nc, half, cw), BF16), vm((3, nc, ny, half, cw), BF16),
        dma((3, nc)), dma((3, nc)), dma((3, nc, ny - 1)), dma((3, nc, ny - 1)), dma((2, nc)), dma((2, nc)),
        vm((groups, slots, fw), BF16), vm((groups, slots, fw), BF16), vm((groups * slots, tok), BF16),
        dma((groups - 1,)), dma((groups - 1,)),
        vm((tok, fw), F32), vm((tok, fw), BF16), vm((tok, ff), F32), vm((tok, ff), BF16), vm((half, d), F32),
        vm(mb, BF16), vm(db, BF16), vm(gb, F32), vm(gb, BF16), vm(zb, BF16), vm(fb, BF16),
        dma((2, nc)), dma((2, nc)), dma((nch,)), dma((nch,)), dma((nch, nsem)), dma((nch, nsem)),
        dma((nch, nsem)), dma((nch, nsem)), dma((nch, nsem)), dma((nch, nsem)),
        vm((tok, d), BF16), dma((1,)), dma((1,)), vm((groups, tok), jnp.int32), vm((groups, tok), jnp.int32),
        dma((nch + 1,)),
    ]
    vspec = pl.BlockSpec(memory_space=pltpu.VMEM)
    aspec = pl.BlockSpec(memory_space=pl.ANY)
    return pl.pallas_call(
        kernel,
        out_shape=(jax.ShapeDtypeStruct(fb if reduce_groups else (d, fw), BF16 if reduce_groups else F32), jax.ShapeDtypeStruct((tok, d), BF16)),
        in_specs=[vspec] * 5 + [aspec] * 3,
        out_specs=(aspec if reduce_groups else vspec, aspec),
        scratch_shapes=scratch,
        compiler_params=pltpu.CompilerParams(
            collective_id=0, has_side_effects=True, vmem_limit_bytes=56 * 1024 * 1024
        ),
    )


def widen(packed, rows, d, fw):
    nch = fw // 128
    nc = d // 256

    def kernel(p_hbm, r_hbm, w_hbm, o_hbm, p, w, r, in_s, out_s):
        ins = [pltpu.make_async_copy(p_hbm.at[c], p.at[c], in_s.at[c]) for c in range(nch)]
        row_in = pltpu.make_async_copy(r_hbm, r, in_s.at[nch])
        row_out = pltpu.make_async_copy(r, o_hbm, out_s.at[nc])
        for c in ins:
            c.start()
        row_in.start()
        for c in ins:
            c.wait()
        row_in.wait()
        row_out.start()
        outs = []
        for j in range(nc):
            for c in range(nch):
                for x in range(2):
                    r0 = j * 256 + x * 128
                    w[r0:r0 + 128, c * 128:(c + 1) * 128] = p[c, x, j * 128:(j + 1) * 128, :].astype(F32)
            part = pl.ds(j * 256, 256)
            outs.append(pltpu.make_async_copy(w.at[part, :], w_hbm.at[part, :], out_s.at[j]))
            outs[-1].start()
        for c in outs:
            c.wait()
        row_out.wait()

    any_ = pl.BlockSpec(memory_space=pl.ANY)
    return pl.pallas_call(
        kernel,
        out_shape=(jax.ShapeDtypeStruct((d, fw), F32), jax.ShapeDtypeStruct(rows.shape, rows.dtype)),
        in_specs=[any_] * 2,
        out_specs=(any_, any_),
        scratch_shapes=[
            pltpu.VMEM(packed.shape, BF16), pltpu.VMEM((d, fw), F32), pltpu.VMEM(rows.shape, BF16),
            pltpu.SemaphoreType.DMA((nch + 1,)), pltpu.SemaphoreType.DMA((nc + 1,)),
        ],
    )(packed, rows)


def solution(mesh):
    groups = mesh.shape["group"]
    tensors = mesh.shape["tensor"]

    def per_device(student_in, teacher_feat, owner, slot_row, w_up, b_up, w_down, w_adapt):
        tok, d = student_in.shape
        fw = teacher_feat.shape[1]
        ff = w_up.shape[1]
        reduce_groups = groups % 2 == 0 and d % (groups * 16) == 0 and fw % 128 == 0
        call = make_kernel(groups, tensors, tok, d, ff, fw, reduce_groups)
        grad_adapt, input_grad = call(
            student_in, teacher_feat, owner, slot_row, b_up, w_up, w_down, w_adapt,
        )
        if reduce_groups:
            grad_adapt, input_grad = widen(grad_adapt, input_grad, d, fw)
        else:
            grad_adapt = lax.psum(grad_adapt, "group") / math.sqrt(tok * groups)
        return grad_adapt, input_grad

    return jax.shard_map(
        per_device,
        mesh=mesh,
        in_specs=(
            P("group", None),
            P("group", "tensor"),
            P(),
            P(),
            P(None, "tensor"),
            P("tensor"),
            P("tensor", None),
            P(None, "tensor"),
        ),
        out_specs=(P(None, "tensor"), P("group", None)),
        check_vma=False,
    )
```

time: 60.1 us -> 57.1 us (0.950)
  other arithmetic: 2.66 us -> 0 us
  Pallas kernels: 55.3 us -> 56.3 us
  local copies, waits for them, and re-layouts: 0.78 us -> 0 us
    pallas_call x0 -> x1, Pallas kernels: none -> 2.84 us  [widen(): pl.pallas_call(kernel, out_shape=(jax.ShapeDtypeStruct((d, fw), F32), jax...]
    convert_element_type x1 -> x0, other arithmetic: 2.66 us -> none  [per_device(): grad_adapt = grad_adapt.astype(F32)]
    pallas_call x1, Pallas kernels: 55.3 us -> 53.5 us  [per_device(): call(student_in, teacher_feat, owner, slot_row, b_up, w_up, w_down, w_adapt)]
    unnamed x3 -> x0, local copies, waits for them, and re-layouts: 0.78 us -> none
where the time goes in v3:
time: 57.1 us; the launch traced here: 57 us
  Pallas kernels  56.3 us (99%)
  between operations  0.64 us (1%)
    pallas_call x1, Pallas kernels, per_device(): call(student_in, teacher_feat, owner, slot_row, b_up, w_up, w_down, w_adapt)  53.5 us
    pallas_call x1, Pallas kernels, widen(): pl.pallas_call(kernel, out_shape=(jax.ShapeDtypeStruct((d, fw), F32), jax...  2.84 us

profile of v3, /device:TPU:0, one launch (start us, length us, event | category | flops | bytes accessed | tf_op | source)
XLA Modules:
  0.0 57.0 jit_solution(1647227617906548704)
XLA Ops:
  0.6 53.5 %shard_map.95 = (bf16[3,2,640,128]{3,2,1,0:T(8,128)(2,1)}, bf16[192,1280]{1,0:T(8,128)(2,1)}) custom-call(bf16[192,1280]{1,0:T(8,128)(2,1)} %x_ref.1, bf16[192,384]{1,0:T(8,128)(2,1)} %teach_ref.1, s32[1536]{0:T(1024)} %owner_in.1, s32[1536]{0:T(1024)} %slot_in.1, f32[1280]{0:T(1024)} %b_ref.1, bf16[1280,1280]{1,0:T(8,128)(2,1)} %wup_hbm.1, ...), custom_call_target="tpu_custom_call" | custom-call | tf_op jit(solution)/shard_map/pallas_call | solution.py:410
  54.1 2.8 %shard_map.96 = (f32[1280,384]{1,0:T(8,128)}, bf16[192,1280]{1,0:T(8,128)(2,1)}) custom-call(bf16[3,2,640,128]{3,2,1,0:T(8,128)(2,1)} %get-tuple-element.4.p_hbm, bf16[192,1280]{1,0:T(8,128)(2,1)} %get-tuple-element.5.r_hbm), custom_call_target="tpu_custom_call" | custom-call | tf_op jit(solution)/shard_map/pallas_call | solution.py:388
